TPU v7x, 32 devices: a whole 2x2x4 slice. The times are simulated.
32 devices in a mesh: dp: 8 (over z, x), tensor: 4 (over y, core).
Axes of the slice: x: 2, y: 2, z: 4, core: 2. Of those that a mesh axis runs over, the one named last changes fastest.
Arguments:
- layer_input: bfloat16 [4096, 768], P('dp', 'tensor'), may hold values from -6 to 6
- segment_ids: int32 [8, 512], P('dp'), may hold values from 0 to 15, never falling along the last dimension, each value on 1 to 256 neighbouring positions
- triple_weight: bfloat16 [768, 3, 768], P(None, None, 'tensor'), may hold values from -0.21875 to 0.21875
- query_value_bias: float32 [2, 768], P(None, 'tensor'), may hold values from -3 to 3
- output_weight: bfloat16 [768, 768], P('tensor'), may hold values from -0.875 to 0.875
- output_bias: float32 [768], P('tensor'), may hold values from -3 to 3
- norm_gain: float32 [768], P('tensor'), may hold values from 0.5 to 1.5
- norm_shift: float32 [768], P('tensor'), may hold values from -3 to 3
- expand_weight: bfloat16 [768, 3072], P(None, 'tensor'), may hold values from -0.21875 to 0.21875
- expand_bias: float32 [3072], P('tensor'), may hold values from -3 to 3
- reduce_weight: bfloat16 [3072, 768], P('tensor'), may hold values from -0.109375 to 0.109375
- reduce_bias: float32 [768], P('tensor'), may hold values from -3 to 3
- final_gain: float32 [768], P('tensor'), may hold values from 0.5 to 1.5
- final_shift: float32 [768], P('tensor'), may hold values from -3 to 3
- cotangent: bfloat16 [4096, 768], P('dp', 'tensor'), may hold values from -6 to 6
Outputs:
- layer_output: bfloat16 [4096, 768], P('dp', 'tensor')
- input_grad: float32 [4096, 768], P('dp', 'tensor')
- triple_grad: float32 [768, 3, 768], P(None, None, 'tensor')
- query_value_grad: float32 [2, 768], P(None, 'tensor')
- output_weight_grad: float32 [768, 768], P('tensor')
- output_bias_grad: float32 [768], P('tensor')
- norm_gain_grad: float32 [768], P('tensor')
- norm_shift_grad: float32 [768], P('tensor')
- expand_weight_grad: float32 [768, 3072], P(None, 'tensor')
- expand_bias_grad: float32 [3072], P('tensor')
- reduce_weight_grad: float32 [3072, 768], P('tensor')
- reduce_bias_grad: float32 [768], P('tensor')
- final_gain_grad: float32 [768], P('tensor')
- final_shift_grad: float32 [768], P('tensor')
Inputs may be any that keep to these rules, and one draw needn't show every extreme that they name: `segment_ids`: segment numbers never fall along a sequence; each document holds 1 to 256 tokens.
All inputs are finite; a program needn't handle non-finite values.
Results may differ from a plain program's by a relative error of at most 0.012.
The roundings to bfloat16 on the way count: a program that leaves them out, or rounds other values in their place, can miss the bound.
Values may be sent and summed in bfloat16 or wider, within the bound.
A program may use at most 64 MiB of HBM per device.

v0:
```python
import jax
import jax.numpy as jnp
from jax import lax
from jax.sharding import PartitionSpec as P

D = 768
HD = 64
EPS = 1e-06


def gelu_value(pre_act):
    return 0.5 * pre_act * (1.0 + lax.erf(pre_act * 0.7071067811865476))


def gelu_slope(pre_act):
    return (
        0.5 * (1.0 + lax.erf(pre_act * 0.7071067811865476))
        + pre_act * jnp.exp(-0.5 * pre_act * pre_act) * 0.3989422804014327
    )


def norm_forward(hidden, gain, shift):
    row_mean = jnp.mean(hidden, axis=-1, keepdims=True)
    centred = hidden - row_mean
    inverse = lax.rsqrt(jnp.mean(centred * centred, axis=-1, keepdims=True) + EPS)
    normed = centred * inverse
    return (normed * gain + shift, normed, inverse)


def norm_backward(upstream, normed, inverse, gain):
    scaled = upstream * gain
    first_mean = jnp.mean(scaled, axis=-1, keepdims=True)
    second_mean = jnp.mean(scaled * normed, axis=-1, keepdims=True)
    return inverse * (scaled - first_mean - normed * second_mean)


def sum_rows(partial):
    return lax.psum_scatter(
        partial.astype(jnp.bfloat16), "tensor", scatter_dimension=0, tiled=True
    ).astype(jnp.float32)


def all_rows(piece):
    return lax.all_gather(piece, "tensor", axis=0, tiled=True)


def column_sum(rows):
    return jnp.sum(rows, axis=0)


def tall_dot(left, right):
    return lax.dot_general(
        left, right, (((0,), (0,)), ((), ())), preferred_element_type=jnp.float32
    )


def wide_dot(left, right):
    return lax.dot_general(
        left, right, (((1,), (1,)), ((), ())), preferred_element_type=jnp.float32
    )


def masked_scores(query_part, key_part, segment_row, head_scale):
    scores = (
        jnp.einsum("qhd,khd->hqk", query_part, key_part, preferred_element_type=jnp.float32)
        * head_scale
    )
    allowed = segment_row[:, None] == segment_row[None, :]
    return jnp.where(allowed[None], scores, -jnp.inf)


def per_device(
    layer_input,
    segment_ids,
    triple_weight,
    query_value_bias,
    output_weight,
    output_bias,
    norm_gain,
    norm_shift,
    expand_weight,
    expand_bias,
    reduce_weight,
    reduce_bias,
    final_gain,
    final_shift,
    cotangent,
):
    seq_len = segment_ids.shape[1]
    tok_count = segment_ids.shape[0] * seq_len
    local_width = triple_weight.shape[2]
    local_heads = local_width // HD
    head_scale = HD ** (-0.5)
    groups = lax.axis_size("tensor")
    rank = lax.axis_index("tensor")
    block = tok_count // groups
    both = lax.all_gather(
        jnp.concatenate([layer_input, cotangent], axis=0), "tensor", axis=1, tiled=True
    )
    gathered = both[:tok_count]
    own_input = lax.dynamic_slice_in_dim(both, rank * block, block, 0).astype(jnp.float32)
    upstream = lax.dynamic_slice_in_dim(both, tok_count + rank * block, block, 0).astype(
        jnp.float32
    )
    vectors = lax.all_gather(
        jnp.stack([output_bias, norm_gain, norm_shift, reduce_bias, final_gain, final_shift]),
        "tensor",
        axis=1,
        tiled=True,
    )
    output_bias, norm_gain, norm_shift, reduce_bias, final_gain, final_shift = [
        vectors[i] for i in range(6)
    ]
    projected = jnp.einsum(
        "td,dcf->tcf", gathered, triple_weight, preferred_element_type=jnp.float32
    )
    query_half = (
        (projected[:, 0] + query_value_bias[0])
        .astype(jnp.bfloat16)
        .reshape(seq_len, local_heads, HD)
    )
    key_half = projected[:, 1].astype(jnp.bfloat16).reshape(seq_len, local_heads, HD)
    value_half = (
        (projected[:, 2] + query_value_bias[1])
        .astype(jnp.bfloat16)
        .reshape(seq_len, local_heads, HD)
    )
    scores = masked_scores(query_half, key_half, segment_ids[0], head_scale)
    top = jnp.max(scores, axis=-1, keepdims=True)
    log_total = top + jnp.log(jnp.sum(jnp.exp(scores - top), axis=-1, keepdims=True))
    probs_half = jnp.exp(scores - log_total).astype(jnp.bfloat16)
    context = jnp.einsum(
        "hqk,khd->qhd", probs_half, value_half, preferred_element_type=jnp.float32
    ).astype(jnp.bfloat16)
    context_flat = context.reshape(tok_count, local_width)
    first_sum = (
        own_input
        + sum_rows(jnp.dot(context_flat, output_weight, preferred_element_type=jnp.float32))
        + output_bias
    )
    attended, normed_one, inv_one = norm_forward(first_sum, norm_gain, norm_shift)
    attended_half = all_rows(attended.astype(jnp.bfloat16))
    pre_act = (
        jnp.dot(attended_half, expand_weight, preferred_element_type=jnp.float32) + expand_bias
    )
    activated = gelu_value(pre_act).astype(jnp.bfloat16)
    second_sum = (
        attended
        + sum_rows(jnp.dot(activated, reduce_weight, preferred_element_type=jnp.float32))
        + reduce_bias
    )
    out_f, normed_two, inv_two = norm_forward(second_sum, final_gain, final_shift)
    layer_output = lax.all_to_all(
        out_f.astype(jnp.bfloat16), "tensor", split_axis=1, concat_axis=0, tiled=True
    )
    final_gain_grad = column_sum(upstream * normed_two)
    final_shift_grad = column_sum(upstream)
    second_grad = norm_backward(upstream, normed_two, inv_two, final_gain)
    second_half = all_rows(second_grad.astype(jnp.bfloat16))
    reduce_weight_grad = tall_dot(activated, second_half)
    reduce_bias_grad = column_sum(second_grad)
    act_grad = wide_dot(second_half, reduce_weight) * gelu_slope(pre_act)
    act_half = act_grad.astype(jnp.bfloat16)
    expand_weight_grad = tall_dot(attended_half, act_half)
    expand_bias_grad = column_sum(act_grad)
    feed_sum = lax.psum(
        jnp.concatenate([reduce_weight_grad, expand_weight_grad], axis=0).astype(jnp.bfloat16), "dp"
    )
    split = reduce_weight_grad.shape[0]
    attended_grad = second_grad + sum_rows(wide_dot(act_half, expand_weight))
    norm_gain_grad = column_sum(attended_grad * normed_one)
    norm_shift_grad = column_sum(attended_grad)
    first_grad = norm_backward(attended_grad, normed_one, inv_one, norm_gain)
    first_half = all_rows(first_grad.astype(jnp.bfloat16))
    output_weight_grad = tall_dot(context_flat, first_half)
    output_bias_grad = column_sum(first_grad)
    grad_part = (
        wide_dot(first_half, output_weight).astype(jnp.bfloat16).reshape(seq_len, local_heads, HD)
    )
    scores = masked_scores(query_half, key_half, segment_ids[0], head_scale)
    probs = jnp.exp(scores - log_total)
    probs_half = probs.astype(jnp.bfloat16)
    value_grad = jnp.einsum(
        "hqk,qhd->khd", probs_half, grad_part, preferred_element_type=jnp.float32
    ).reshape(tok_count, local_width)
    prob_grad = jnp.einsum(
        "qhd,khd->hqk", grad_part, value_half, preferred_element_type=jnp.float32
    )
    delta = jnp.einsum("qhd,qhd->hq", grad_part.astype(jnp.float32), context.astype(jnp.float32))
    score_grad = (probs * (prob_grad - delta[:, :, None]) * head_scale).astype(jnp.bfloat16)
    query_grad = jnp.einsum(
        "hqk,khd->qhd", score_grad, key_half, preferred_element_type=jnp.float32
    ).reshape(tok_count, local_width)
    key_grad = jnp.einsum(
        "hqk,qhd->khd", score_grad, query_half, preferred_element_type=jnp.float32
    ).reshape(tok_count, local_width)
    triple_half = jnp.stack([query_grad, key_grad, value_grad], axis=1).astype(jnp.bfloat16)
    triple_grad = jnp.einsum(
        "td,tcf->dcf", gathered, triple_half, preferred_element_type=jnp.float32
    )
    input_terms = jnp.einsum(
        "tcf,dcf->td", triple_half, triple_weight, preferred_element_type=jnp.float32
    )
    smalls = jnp.stack(
        [
            output_bias_grad,
            norm_gain_grad,
            norm_shift_grad,
            reduce_bias_grad,
            final_gain_grad,
            final_shift_grad,
        ]
    )
    own_rows = lax.dynamic_slice_in_dim(input_terms, rank * block, block, 0) + first_grad
    input_terms = lax.dynamic_update_slice_in_dim(input_terms, own_rows, rank * block, 0)
    shares = lax.psum_scatter(
        jnp.concatenate([input_terms, smalls, jnp.zeros((10, D), jnp.float32)], axis=0).astype(
            jnp.bfloat16
        ),
        "tensor",
        scatter_dimension=1,
        tiled=True,
    ).astype(jnp.float32)
    input_grad = shares[:tok_count]
    pieces = [
        triple_grad,
        output_weight_grad,
        expand_bias_grad,
        jnp.sum(query_grad, axis=0),
        jnp.sum(value_grad, axis=0),
        shares[tok_count : tok_count + 6],
    ]
    packed = jnp.concatenate([p.reshape(-1, local_width) for p in pieces], axis=0)
    packed, feed_sum = lax.optimization_barrier((packed.astype(jnp.bfloat16), feed_sum))
    packed = lax.psum(packed, "dp").astype(jnp.float32)
    reduce_weight_grad = feed_sum[:split].astype(jnp.float32)
    expand_weight_grad = feed_sum[split:].astype(jnp.float32)
    outs, at = ([], 0)
    for p in pieces:
        count = p.size // local_width
        outs.append(packed[at : at + count].reshape(p.shape))
        at += count
    triple_grad, output_weight_grad, expand_bias_grad, query_sum, value_sum, small_sums = outs
    return (
        layer_output,
        input_grad,
        triple_grad,
        jnp.stack([query_sum, value_sum]),
        output_weight_grad,
        small_sums[0],
        small_sums[1],
        small_sums[2],
        expand_weight_grad,
        expand_bias_grad,
        reduce_weight_grad,
        small_sums[3],
        small_sums[4],
        small_sums[5],
    )


def solution(mesh):
    in_specs = (
        P("dp", "tensor"),
        P("dp", None),
        P(None, None, "tensor"),
        P(None, "tensor"),
        P("tensor", None),
        P("tensor"),
        P("tensor"),
        P("tensor"),
        P(None, "tensor"),
        P("tensor"),
        P("tensor", None),
        P("tensor"),
        P("tensor"),
        P("tensor"),
        P("dp", "tensor"),
    )
    out_specs = (
        P("dp", "tensor"),
        P("dp", "tensor"),
        P(None, None, "tensor"),
        P(None, "tensor"),
        P("tensor", None),
        P("tensor"),
        P("tensor"),
        P("tensor"),
        P(None, "tensor"),
        P("tensor"),
        P("tensor", None),
        P("tensor"),
        P("tensor"),
        P("tensor"),
    )
    return jax.shard_map(
        per_device, mesh=mesh, in_specs=in_specs, out_specs=out_specs, check_vma=False
    )
```

profile of v0, /device:TPU:0, one launch (start us, length us, event | category | flops | bytes accessed | tf_op | source)
XLA Modules:
  0.0 413.7 jit_solution(5651966376495020116)
XLA Ops:
  7.2 1.9 pad_maximum_fusion.2
  11.1 21.4 %all-gather.3.cloned.1.call-done = bf16[1024,768]{0,1:T(8,128)(2,1)} async-done(((bf16[1024,192]{0,1:T(8,128)(2,1)}), bf16[1024,768]{0,1:T(8,128)(2,1)}) %all-gather.3.cloned.1.call-update) | async-done | bytes 1572880 | tf_op jit(solution)/shard_map/all_gather | solution.py:97
  32.6 2.0 fusion.7
  39.7 5.2 %all-gather = f32[4,192,6]{1,2,0:T(8,128)S(1)} all-gather(f32[1,192,6]{1,2,0:T(8,128)S(1)} %bitcast.109), channel_id=1, replica_groups=mesh['dp'=8,'tensor'=4] {'tensor'}, dimensions={0}, use_global_device_ids=true | all-gather | bytes 23040 | tf_op jit(solution)/shard_map/all_gather | solution.py:105
  46.4 16.6 %reduce-scatter.7.cloned.1.call-done = bf16[128,768]{1,0:T(8,128)(2,1)} async-done(((bf16[512,768]{1,0:T(8,128)(2,1)}), bf16[128,768]{1,0:T(8,128)(2,1)}) %reduce-scatter.7.cloned.1.call-update) | async-done | bytes 196624 | tf_op jit(solution)/shard_map/reduce_scatter | solution.py:38
  66.2 8.2 %all_gather.17 = bf16[512,768]{1,0:T(8,128)(2,1)S(1)} all-gather(bf16[128,768]{1,0:T(8,128)(2,1)S(1)} %fusion.21), channel_id=1, replica_groups=mesh['dp'=8,'tensor'=4] {'tensor'}, dimensions={0}, use_global_device_ids=true | all-gather | bytes 983040 | tf_op jit(solution)/shard_map/all_gather | solution.py:44
  74.5 2.0 multiply_convert_fusion.1
  79.3 23.6 %reduce-scatter.9.cloned.1.call-done = bf16[128,768]{1,0:T(8,128)(2,1)} async-done(((bf16[512,768]{1,0:T(8,128)(2,1)}), bf16[128,768]{1,0:T(8,128)(2,1)}) %reduce-scatter.9.cloned.1.call-update) | async-done | bytes 196624 | tf_op jit(solution)/shard_map/reduce_scatter | solution.py:38
  105.5 8.2 %all_gather.18 = bf16[512,768]{1,0:T(8,128)(2,1)S(1)} all-gather(bf16[128,768]{1,0:T(8,128)(2,1)S(1)} %get-tuple-element.94), channel_id=1, replica_groups=mesh['dp'=8,'tensor'=4] {'tensor'}, dimensions={0}, use_global_device_ids=true | all-gather | bytes 983040 | tf_op jit(solution)/shard_map/all_gather | solution.py:44
  118.0 23.7 %reduce-scatter.11.cloned.1.call-done = bf16[128,768]{1,0:T(8,128)(2,1)} async-done(((bf16[512,768]{1,0:T(8,128)(2,1)}), bf16[128,768]{1,0:T(8,128)(2,1)}) %reduce-scatter.11.cloned.1.call-update) | async-done | bytes 196624 | tf_op jit(solution)/shard_map/reduce_scatter | solution.py:38
  144.3 8.5 %all_gather.19 = bf16[512,768]{1,0:T(8,128)(2,1)S(1)} all-gather(bf16[128,768]{1,0:T(8,128)(2,1)S(1)} %convert_element_type.106), channel_id=1, replica_groups=mesh['dp'=8,'tensor'=4] {'tensor'}, dimensions={0}, use_global_device_ids=true | all-gather | bytes 983040 | tf_op jit(solution)/shard_map/all_gather | solution.py:44
  159.4 3.1 concatenate.16
  163.9 2.3 convolution_convert_fusion.1
  172.2 2.5 copy.72
  174.8 2.2 reshape.172
  178.9 10.0 %reduce-scatter.13.cloned.1.call-done = bf16[192,528]{1,0:T(8,128)(2,1)} async-done(((bf16[768,528]{1,0:T(8,128)(2,1)}), bf16[192,528]{1,0:T(8,128)(2,1)}) %reduce-scatter.13.cloned.1.call-update) | async-done | bytes 202768
  189.8 6.7 %concatenate.17 = bf16[3084,192]{1,0:T(8,128)(2,1)} concatenate(bf16[2304,192]{1,0:T(8,128)(2,1)S(1)} %copy-done.5, bf16[768,192]{1,0:T(8,128)(2,1)S(1)} %reshape.173, bf16[4,192]{1,0:T(4,128)(2,1)S(1)} %reshape.174, bf16[1,192]{1,0:T(2,128)(2,1)S(1)} %reshape.175, bf16[1,192]{1,0:T(2,128)(2,1)S(1)} %reshape.176, bf16[6,192]{1,0:T(8,128)(2,1)S(1)} %copy.93), dimensions={0} | concatenate | bytes 2368512 | tf_op jit(solution)/shard_map/concatenate | solution.py:233
  196.5 105.1 %all-reduce.3.cloned.1.call-done = bf16[1536,768]{1,0:T(8,128)(2,1)} async-done(((bf16[1536,768]{1,0:T(8,128)(2,1)}), bf16[1536,768]{1,0:T(8,128)(2,1)}) %all-reduce.3.cloned.1.call-update) | async-done | bytes 2359312 | tf_op jit(solution)/shard_map/psum | solution.py:166
  301.7 1.9 copy.65
  303.6 8.7 %all_to_all.19 = bf16[128,4,192]{0,2,1:T(8,128)(2,1)S(1)} all-to-all(bf16[128,4,192]{0,2,1:T(8,128)(2,1)} %bitcast.101), channel_id=1, replica_groups=mesh['dp'=8,'tensor'=4] {'tensor'}, dimensions={1} | all-to-all | bytes 393216 | tf_op jit(solution)/shard_map/all_to_all | solution.py:153
  318.1 2.5 slice_convert_fusion
  320.7 74.8 %all-reduce.5.cloned.1.call-done = bf16[3084,192]{1,0:T(8,128)(2,1)} async-done(((bf16[3084,192]{1,0:T(8,128)(2,1)}), bf16[3084,192]{1,0:T(8,128)(2,1)}) %all-reduce.5.cloned.1.call-update) | async-done | bytes 1184272 | tf_op jit(solution)/shard_map/psum | solution.py:235
  396.9 2.6 reshape.177
  399.5 4.3 %copy.74 = f32[768,3,192]{0,2,1:T(8,128)} copy(f32[768,3,192]{2,1,0:T(4,128)} %reshape.177) | data formatting | bytes 3538944
  (160 shorter events, 50.9 us)
Async XLA Ops:
  7.2 67.3 %copy-start = (bf16[768,768]{1,0:T(8,128)(2,1)S(1)}, bf16[768,768]{1,0:T(8,128)(2,1)}, u32[]{:S(2)}) copy-start(bf16[768,768]{1,0:T(8,128)(2,1)} %param.23) | copy-start | bytes 3538948
  7.2 25.4 %all-gather.3.cloned.1.call-start = ((), (), s32[]{:S(2)}) async-start(), calls=%async_computation.5 | async-start | bytes 1966080 | tf_op jit(solution)/shard_map/all_gather | solution.py:97
  9.2 53.8 %reduce-scatter.7.cloned.1.call-start = ((), (), s32[]{:S(2)}) async-start(), calls=%async_computation.6 | async-start | bytes 983040 | tf_op jit(solution)/shard_map/reduce_scatter | solution.py:38
  38.1 115.1 %copy-start.8 = (bf16[3,64,512]{2,1,0:T(8,128)(2,1)}, bf16[3,64,512]{2,1,0:T(8,128)(2,1)S(1)}, u32[]{:S(2)}) copy-start(bf16[3,64,512]{2,1,0:T(8,128)(2,1)S(1)} %convolution_convert_fusion.7) | copy-start | bytes 589828
  39.5 63.4 %reduce-scatter.9.cloned.1.call-start = ((), (), s32[]{:S(2)}) async-start(), calls=%async_computation.7 | async-start | bytes 983040 | tf_op jit(solution)/shard_map/reduce_scatter | solution.py:38
  46.2 28.2 %copy-start.29 = (f32[768]{0:T(1024)S(1)}, f32[768]{0:T(1024)}, u32[]{:S(2)}) copy-start(f32[768]{0:T(1024)} %param.24) | copy-start | bytes 9220
  74.5 2.0 copy-start.13
  74.5 3.0 copy-start.27
  77.4 25.5 %copy-start.3 = (bf16[128,768]{1,0:T(8,128)(2,1)S(1)}, bf16[128,768]{1,0:T(8,128)(2,1)}, u32[]{:S(2)}) copy-start(bf16[128,768]{1,0:T(8,128)(2,1)} %reduce-scatter.7.cloned.1.call-done) | copy-start | bytes 589828
  79.1 62.7 %reduce-scatter.11.cloned.1.call-start = ((), (), s32[]{:S(2)}) async-start(), calls=%async_computation.8 | async-start | bytes 983040 | tf_op jit(solution)/shard_map/reduce_scatter | solution.py:38
  104.3 9.4 %copy-start.28 = (bf16[768,768]{1,0:T(8,128)(2,1)S(1)}, bf16[768,768]{1,0:T(8,128)(2,1)}, u32[]{:S(2)}) copy-start(bf16[768,768]{1,0:T(8,128)(2,1)} %param.25) | copy-start | bytes 3538948
  104.3 9.4 %copy-start.33 = (f32[512,768]{1,0:T(8,128)S(1)}, f32[512,768]{1,0:T(8,128)}, u32[]{:S(2)}) copy-start(f32[512,768]{1,0:T(8,128)} %get-tuple-element.117) | copy-start | bytes 4718596
  118.0 70.9 %reduce-scatter.13.cloned.1.call-start = ((), (), s32[]{:S(2)}) async-start(), calls=%async_computation.11 | async-start | bytes 1228800
  143.1 10.3 %copy-start.17 = (f32[512,1,192]{0,2,1:T(8,128)S(1)}, f32[512,1,192]{0,2,1:T(8,128)}, u32[]{:S(2)}) copy-start(f32[512,1,192]{0,2,1:T(8,128)} %copy-done.16) | copy-start | bytes 1179652
  144.3 9.1 %copy-start.2 = (f32[3,512,512]{1,2,0:T(8,128)S(1)}, f32[3,512,512]{1,2,0:T(8,128)}, u32[]{:S(2)}) copy-start(f32[3,512,512]{1,2,0:T(8,128)} %copy-done.1) | copy-start | bytes 9437188
  155.2 2.3 copy-start.11
  163.8 2.4 copy-start.14
  163.9 2.4 copy-start.32
  163.9 137.8 %all-reduce.3.cloned.1.call-start = ((), (), s32[]{:S(2)}) async-start(), calls=%async_computation.9 | async-start | bytes 4718592 | tf_op jit(solution)/shard_map/psum | solution.py:166
  168.6 2.0 copy-start.6
  168.6 226.9 %all-reduce.5.cloned.1.call-start = ((), (), s32[]{:S(2)}) async-start(), calls=%async_computation.10 | async-start | bytes 3162112 | tf_op jit(solution)/shard_map/psum | solution.py:235
  177.0 12.8 %copy-start.5 = (bf16[2304,192]{1,0:T(8,128)(2,1)S(1)}, bf16[2304,192]{1,0:T(8,128)(2,1)}, u32[]{:S(2)}) copy-start(bf16[2304,192]{1,0:T(8,128)(2,1)} %reshape.172) | copy-start | bytes 2654212
  301.7 16.5 %copy-start.7 = (bf16[1536,768]{1,0:T(8,128)(2,1)S(1)}, bf16[1536,768]{1,0:T(8,128)(2,1)}, u32[]{:S(2)}) copy-start(bf16[1536,768]{1,0:T(8,128)(2,1)} %all-reduce.3.cloned.1.call-done) | copy-start | bytes 7077892
  399.5 4.3 %copy-start.4 = (bf16[3084,192]{1,0:T(8,128)(2,1)S(1)}, bf16[3084,192]{1,0:T(8,128)(2,1)}, u32[]{:S(2)}) copy-start(bf16[3084,192]{1,0:T(8,128)(2,1)} %all-reduce.5.cloned.1.call-done) | copy-start | bytes 3552772
  (17 other events, 23.2 us)
Sparse Core Ops, SparseCore 0:
  10.2 22.3 all-gather.2
  39.7 23.2 reduce-scatter.6
  79.2 23.6 reduce-scatter.8
  118.1 23.6 reduce-scatter.10
  164.0 24.8 reduce-scatter.12
  192.9 108.7 all-reduce.2
  306.2 89.2 all-reduce.4
where the time goes:
time: 415 us; the launch traced here: 414 us
  waiting for transfers between devices  275 us (66%)
  local copies, waits for them, and re-layouts  41.6 us (10%)
  blocking collectives  38.8 us (9%)
  matrix products  22.5 us (5%)
  other arithmetic  20.5 us (5%)
  between operations  14.7 us (4%)
    psum x1, waiting for transfers between devices, per_device(): lax.psum(jnp.concatenate([reduce_weight_grad, expand_weight_grad], axis=0...  105 us
    psum x1, waiting for transfers between devices, per_device(): packed = lax.psum(packed, 'dp').astype(jnp.float32)  74.8 us
    reduce_scatter x3, waiting for transfers between devices, sum_rows(): lax.psum_scatter(partial.astype(jnp.bfloat16), 'tensor', scatter_dimensio...  63.9 us
    all_gather x3, blocking collectives, all_rows(): return lax.all_gather(piece, 'tensor', axis=0, tiled=True)  24.9 us
    all_gather x1, waiting for transfers between devices, per_device(): lax.all_gather(jnp.concatenate([layer_input, cotangent], axis=0), 'tensor...  21.4 us
    unnamed x76, local copies, waits for them, and re-layouts  13.2 us
    unnamed x8, waiting for transfers between devices  10.1 us
    all_to_all x1, blocking collectives, per_device(): lax.all_to_all(out_f.astype(jnp.bfloat16), 'tensor', split_axis=1, concat...  8.67 us
  transfers between devices with their start and end apart: 7, of which 7 were waited for; matrix products, arithmetic and copies ran while one was open for 9% of the time, Pallas kernels for 0%

commit v1 on v0

--- a/solution.py
+++ b/solution.py
@@ -6,6 +6,28 @@
 D = 768
 HD = 64
 EPS = 1e-06
+
+
+def joined_along(blocks, dim):
+    blocks = jnp.moveaxis(blocks, 0, dim)
+    shape = blocks.shape
+    return blocks.reshape(*shape[:dim], shape[dim] * shape[dim + 1], *shape[dim + 2 :])
+
+
+def doubled(x, axis):
+    size = lax.axis_size(axis)
+    tiles = x[None]
+    for level in range(size.bit_length() - 1):
+        stride = 1 << level
+        other = lax.ppermute(tiles, axis, [(i, i ^ stride) for i in range(size)])
+        both = jnp.stack([tiles, other])
+        upper = lax.axis_index(axis) >> level & 1
+        tiles = jnp.where(upper == 0, both, both[::-1]).reshape(-1, *x.shape)
+    return tiles
+
+
+def doubled_up(value, axis, dim):
+    return joined_along(doubled(value, axis), dim)
 
 
 def gelu_value(pre_act):
@@ -41,7 +63,7 @@
 
 
 def all_rows(piece):
-    return lax.all_gather(piece, "tensor", axis=0, tiled=True)
+    return doubled_up(piece, "tensor", 0)
 
 
 def column_sum(rows):

time: 415 us -> 428 us (1.031)
  waiting for transfers between devices: 275 us -> 319 us
  blocking collectives: 38.8 us -> 13.2 us
    ppermute x0 -> x6, waiting for transfers between devices: none -> 36.9 us  [doubled(): other = lax.ppermute(tiles, axis, [(i, i ^ stride) for i in range(size)])]
    all_gather x3 -> x0, blocking collectives: 24.9 us -> none  [all_rows(): return lax.all_gather(piece, 'tensor', axis=0, tiled=True)]
    psum x1, waiting for transfers between devices: 74.8 us -> 81.3 us  [per_device(): packed = lax.psum(packed, 'dp').astype(jnp.float32)]
    unnamed x76 -> x78, local copies, waits for them, and re-layouts: 13.2 us -> 15.2 us
  transfers between devices with their start and end apart: 7 -> 13, of which waited for: 7 -> 13; matrix products, arithmetic and copies ran while one was open for 9% -> 6% of each run, Pallas kernels for 0% -> 0%
where the time goes in v1:
time: 428 us; the launch traced here: 427 us
  waiting for transfers between devices  319 us (75%)
  local copies, waits for them, and re-layouts  37.6 us (9%)
  other arithmetic  20.2 us (5%)
  matrix products  20.1 us (5%)
  between operations  14.8 us (3%)
  blocking collectives  13.2 us (3%)
    psum x1, waiting for transfers between devices, per_device(): lax.psum(jnp.concatenate([reduce_weight_grad, expand_weight_grad], axis=0...  105 us
    psum x1, waiting for transfers between devices, per_device(): packed = lax.psum(packed, 'dp').astype(jnp.float32)  81.3 us
    reduce_scatter x3, waiting for transfers between devices, sum_rows(): lax.psum_scatter(partial.astype(jnp.bfloat16), 'tensor', scatter_dimensio...  63 us
    ppermute x6, waiting for transfers between devices, doubled(): other = lax.ppermute(tiles, axis, [(i, i ^ stride) for i in range(size)])  36.9 us
    all_gather x1, waiting for transfers between devices, per_device(): lax.all_gather(jnp.concatenate([layer_input, cotangent], axis=0), 'tensor...  21.4 us
    unnamed x78, local copies, waits for them, and re-layouts  15.2 us
    unnamed x8, waiting for transfers between devices  11.2 us
  transfers between devices with their start and end apart: 13, of which 13 were waited for; matrix products, arithmetic and copies ran while one was open for 6% of the time, Pallas kernels for 0%

profile of v1, /device:TPU:0, one launch (start us, length us, event | category | flops | bytes accessed | tf_op | source)
XLA Modules:
  0.0 426.7 jit_solution(13886052901047746328)
XLA Ops:
  7.2 1.9 pad_maximum_fusion.5
  11.1 21.4 %all-gather.3.cloned.1.call-done = bf16[1024,768]{0,1:T(8,128)(2,1)} async-done(((bf16[1024,192]{0,1:T(8,128)(2,1)}), bf16[1024,768]{0,1:T(8,128)(2,1)}) %all-gather.3.cloned.1.call-update) | async-done | bytes 1572880 | tf_op jit(solution)/shard_map/all_gather | solution.py:119
  32.6 2.0 fusion.7
  39.7 5.2 %all-gather = f32[4,192,6]{1,2,0:T(8,128)S(1)} all-gather(f32[1,192,6]{1,2,0:T(8,128)S(1)} %bitcast.162), channel_id=1, replica_groups=mesh['dp'=8,'tensor'=4] {'tensor'}, dimensions={0}, use_global_device_ids=true | all-gather | bytes 23040 | tf_op jit(solution)/shard_map/all_gather | solution.py:127
  46.4 16.6 %reduce-scatter.7.cloned.1.call-done = bf16[128,768]{1,0:T(8,128)(2,1)} async-done(((bf16[512,768]{1,0:T(8,128)(2,1)}), bf16[128,768]{1,0:T(8,128)(2,1)}) %reduce-scatter.7.cloned.1.call-update) | async-done | bytes 196624 | tf_op jit(solution)/shard_map/reduce_scatter | solution.py:60
  68.9 11.1 %collective-permute-done.1 = bf16[2,128,768]{2,1,0:T(8,128)(2,1)S(1)} collective-permute-done((bf16[2,128,768]{2,1,0:T(8,128)(2,1)}, bf16[2,128,768]{2,1,0:T(8,128)(2,1)S(1)}, u32[]{:S(2)}, u32[]{:S(2)}) %collective-permute-start.1) | collective-permute-done | bytes 393248 | tf_op jit(solution)/shard_map/ppermute | solution.py:22
  80.7 2.0 multiply_convert_fusion.1
  83.6 1.7 convolution_convert_fusion.3
  85.5 23.2 %reduce-scatter.9.cloned.1.call-done = bf16[128,768]{1,0:T(8,128)(2,1)} async-done(((bf16[512,768]{1,0:T(8,128)(2,1)}), bf16[128,768]{1,0:T(8,128)(2,1)}) %reduce-scatter.9.cloned.1.call-update) | async-done | bytes 196624 | tf_op jit(solution)/shard_map/reduce_scatter | solution.py:60
  113.3 10.8 %collective-permute-done.3 = bf16[2,128,768]{2,1,0:T(8,128)(2,1)S(1)} collective-permute-done((bf16[2,128,768]{2,1,0:T(8,128)(2,1)S(1)}, bf16[2,128,768]{2,1,0:T(8,128)(2,1)S(1)}, u32[]{:S(2)}, u32[]{:S(2)}) %collective-permute-start.3) | collective-permute-done | bytes 393248 | tf_op jit(solution)/shard_map/ppermute | solution.py:22
  128.2 1.7 convolution_convert_fusion.2
  130.2 23.2 %reduce-scatter.11.cloned.1.call-done = bf16[128,768]{1,0:T(8,128)(2,1)} async-done(((bf16[512,768]{1,0:T(8,128)(2,1)}), bf16[128,768]{1,0:T(8,128)(2,1)}) %reduce-scatter.11.cloned.1.call-update) | async-done | bytes 196624 | tf_op jit(solution)/shard_map/reduce_scatter | solution.py:60
  157.9 10.8 %collective-permute-done.5 = bf16[2,128,768]{2,1,0:T(8,128)(2,1)S(1)} collective-permute-done((bf16[2,128,768]{2,1,0:T(8,128)(2,1)S(1)}, bf16[2,128,768]{2,1,0:T(8,128)(2,1)S(1)}, u32[]{:S(2)}, u32[]{:S(2)}) %collective-permute-start.5) | collective-permute-done | bytes 393248 | tf_op jit(solution)/shard_map/ppermute | solution.py:22
  177.3 2.0 convolution_convert_fusion.1
  185.1 2.5 copy.83
  187.6 2.2 reshape.184
  190.7 11.1 %reduce-scatter.13.cloned.1.call-done = bf16[192,528]{1,0:T(8,128)(2,1)} async-done(((bf16[768,528]{1,0:T(8,128)(2,1)}), bf16[192,528]{1,0:T(8,128)(2,1)}) %reduce-scatter.13.cloned.1.call-update) | async-done | bytes 202768
  202.7 6.7 %concatenate.17 = bf16[3084,192]{1,0:T(8,128)(2,1)} concatenate(bf16[2304,192]{1,0:T(8,128)(2,1)S(1)} %copy-done.6, bf16[768,192]{1,0:T(8,128)(2,1)S(1)} %reshape.185, bf16[4,192]{1,0:T(4,128)(2,1)S(1)} %reshape.186, bf16[1,192]{1,0:T(2,128)(2,1)S(1)} %reshape.187, bf16[1,192]{1,0:T(2,128)(2,1)S(1)} %reshape.188, bf16[6,192]{1,0:T(8,128)(2,1)S(1)} %copy.104), dimensions={0} | concatenate | bytes 2368512 | tf_op jit(solution)/shard_map/concatenate | solution.py:255
  209.5 105.1 %all-reduce.3.cloned.1.call-done = bf16[1536,768]{1,0:T(8,128)(2,1)} async-done(((bf16[1536,768]{1,0:T(8,128)(2,1)}), bf16[1536,768]{1,0:T(8,128)(2,1)}) %all-reduce.3.cloned.1.call-update) | async-done | bytes 2359312 | tf_op jit(solution)/shard_map/psum | solution.py:188
  314.8 8.0 %all_to_all.19 = bf16[128,4,192]{0,2,1:T(8,128)(2,1)S(1)} all-to-all(bf16[128,4,192]{0,2,1:T(8,128)(2,1)S(1)} %bitcast.148), channel_id=1, replica_groups=mesh['dp'=8,'tensor'=4] {'tensor'}, dimensions={1} | all-to-all | bytes 393216 | tf_op jit(solution)/shard_map/all_to_all | solution.py:175
  324.6 2.5 slice_convert_fusion
  327.1 81.3 %all-reduce.5.cloned.1.call-done = bf16[3084,192]{1,0:T(8,128)(2,1)} async-done(((bf16[3084,192]{1,0:T(8,128)(2,1)}), bf16[3084,192]{1,0:T(8,128)(2,1)}) %all-reduce.5.cloned.1.call-update) | async-done | bytes 1184272 | tf_op jit(solution)/shard_map/psum | solution.py:257
  409.9 2.6 reshape.189
  412.5 4.4 %copy.85 = f32[768,3,192]{0,2,1:T(8,128)} copy(f32[768,3,192]{2,1,0:T(4,128)} %reshape.189) | data formatting | bytes 3538944
  (184 shorter events, 51.8 us)
Async XLA Ops:
  7.2 73.0 %copy-start = (bf16[768,768]{1,0:T(8,128)(2,1)S(1)}, bf16[768,768]{1,0:T(8,128)(2,1)}, u32[]{:S(2)}) copy-start(bf16[768,768]{1,0:T(8,128)(2,1)} %param.23) | copy-start | bytes 3538948
  7.2 25.4 %all-gather.3.cloned.1.call-start = ((), (), s32[]{:S(2)}) async-start(), calls=%async_computation.5 | async-start | bytes 1966080 | tf_op jit(solution)/shard_map/all_gather | solution.py:119
  9.2 53.8 %reduce-scatter.7.cloned.1.call-start = ((), (), s32[]{:S(2)}) async-start(), calls=%async_computation.6 | async-start | bytes 983040 | tf_op jit(solution)/shard_map/reduce_scatter | solution.py:60
  39.5 69.2 %reduce-scatter.9.cloned.1.call-start = ((), (), s32[]{:S(2)}) async-start(), calls=%async_computation.7 | async-start | bytes 983040 | tf_op jit(solution)/shard_map/reduce_scatter | solution.py:60
  66.2 1.5 collective-permute-start
  68.6 11.4 %collective-permute-start.1 = (bf16[2,128,768]{2,1,0:T(8,128)(2,1)}, bf16[2,128,768]{2,1,0:T(8,128)(2,1)S(1)}, u32[]{:S(2)}, u32[]{:S(2)}) collective-permute-start(bf16[2,128,768]{2,1,0:T(8,128)(2,1)} %get-tuple-element.123), channel_id=1, source_target_pairs={{0,2},{1,3},{2,0},{3,1},{4,6},{5,7},{6,4},{7,5},{8,10},{9,11},{10,... | collective-permute-start | bytes 1179656 | tf_op jit(solution)/shard_map/ppermute | solution.py:22
  80.2 2.5 copy-start.12
  80.7 3.0 copy-start.28
  83.6 25.1 %copy-start.4 = (bf16[128,768]{1,0:T(8,128)(2,1)S(1)}, bf16[128,768]{1,0:T(8,128)(2,1)}, u32[]{:S(2)}) copy-start(bf16[128,768]{1,0:T(8,128)(2,1)} %reduce-scatter.7.cloned.1.call-done) | copy-start | bytes 589828
  85.3 68.1 %reduce-scatter.11.cloned.1.call-start = ((), (), s32[]{:S(2)}) async-start(), calls=%async_computation.8 | async-start | bytes 983040 | tf_op jit(solution)/shard_map/reduce_scatter | solution.py:60
  111.3 1.5 collective-permute-start.2
  112.9 11.2 %collective-permute-start.3 = (bf16[2,128,768]{2,1,0:T(8,128)(2,1)S(1)}, bf16[2,128,768]{2,1,0:T(8,128)(2,1)S(1)}, u32[]{:S(2)}, u32[]{:S(2)}) collective-permute-start(bf16[2,128,768]{2,1,0:T(8,128)(2,1)S(1)} %get-tuple-element.121), channel_id=1, source_target_pairs={{0,2},{1,3},{2,0},{3,1},{4,6},{5,7},{6,4},{7,5},{8,10},{9,11},{10,... | collective-permute-start | bytes 1179656 | tf_op jit(solution)/shard_map/ppermute | solution.py:22
  124.4 2.9 copy-start.14
  129.9 71.9 %reduce-scatter.13.cloned.1.call-start = ((), (), s32[]{:S(2)}) async-start(), calls=%async_computation.11 | async-start | bytes 1228800
  155.8 1.5 collective-permute-start.4
  157.4 11.2 %collective-permute-start.5 = (bf16[2,128,768]{2,1,0:T(8,128)(2,1)S(1)}, bf16[2,128,768]{2,1,0:T(8,128)(2,1)S(1)}, u32[]{:S(2)}, u32[]{:S(2)}) collective-permute-start(bf16[2,128,768]{2,1,0:T(8,128)(2,1)S(1)} %get-tuple-element.117), channel_id=1, source_target_pairs={{0,2},{1,3},{2,0},{3,1},{4,6},{5,7},{6,4},{7,5},{8,10},{9,11},{10,... | collective-permute-start | bytes 1179656 | tf_op jit(solution)/shard_map/ppermute | solution.py:22
  177.2 137.4 %all-reduce.3.cloned.1.call-start = ((), (), s32[]{:S(2)}) async-start(), calls=%async_computation.9 | async-start | bytes 4718592 | tf_op jit(solution)/shard_map/psum | solution.py:188
  181.8 226.7 %all-reduce.5.cloned.1.call-start = ((), (), s32[]{:S(2)}) async-start(), calls=%async_computation.10 | async-start | bytes 3162112 | tf_op jit(solution)/shard_map/psum | solution.py:257
  189.8 12.9 %copy-start.6 = (bf16[2304,192]{1,0:T(8,128)(2,1)S(1)}, bf16[2304,192]{1,0:T(8,128)(2,1)}, u32[]{:S(2)}) copy-start(bf16[2304,192]{1,0:T(8,128)(2,1)} %reshape.184) | copy-start | bytes 2654212
  209.5 105.2 %copy-start.16 = (bf16[128,768]{1,0:T(8,128)(2,1)S(1)}, bf16[128,768]{1,0:T(8,128)(2,1)}, u32[]{:S(2)}) copy-start(bf16[128,768]{1,0:T(8,128)(2,1)} %get-tuple-element.111) | copy-start | bytes 589828
  209.5 114.0 %copy-start.19 = (bf16[192,528]{1,0:T(8,128)(2,1)S(1)}, bf16[192,528]{1,0:T(8,128)(2,1)}, u32[]{:S(2)}) copy-start(bf16[192,528]{1,0:T(8,128)(2,1)} %reduce-scatter.13.cloned.1.call-done) | copy-start | bytes 608260
  314.6 9.9 %copy-start.8 = (bf16[1536,768]{1,0:T(8,128)(2,1)S(1)}, bf16[1536,768]{1,0:T(8,128)(2,1)}, u32[]{:S(2)}) copy-start(bf16[1536,768]{1,0:T(8,128)(2,1)} %all-reduce.3.cloned.1.call-done) | copy-start | bytes 7077892
  412.5 4.4 %copy-start.5 = (bf16[3084,192]{1,0:T(8,128)(2,1)S(1)}, bf16[3084,192]{1,0:T(8,128)(2,1)}, u32[]{:S(2)}) copy-start(bf16[3084,192]{1,0:T(8,128)(2,1)} %all-reduce.5.cloned.1.call-done) | copy-start | bytes 3552772
  412.5 7.4 %copy-start.1 = (bf16[768,768]{1,0:T(8,128)(2,1)S(1)}, bf16[768,768]{1,0:T(8,128)(2,1)}, u32[]{:S(2)}) copy-start(bf16[768,768]{1,0:T(8,128)(2,1)} %param.23) | copy-start | bytes 3538948
  (24 other events, 33.9 us)
Sparse Core Ops, SparseCore 0:
  10.2 22.3 all-gather.2
  39.7 23.2 reduce-scatter.6
  85.4 23.2 reduce-scatter.8
  130.0 23.2 reduce-scatter.10
  177.4 24.4 reduce-scatter.12
  205.9 108.7 all-reduce.2
  319.2 89.2 all-reduce.4
